TPU v7x, 256 devices: a whole 4x4x8 slice. The times are simulated.
256 devices in a mesh: dom: 64 (over y, z, core), col: 4 (over x).
Axes of the slice: x: 4, y: 4, z: 8, core: 2. Of those that a mesh axis runs over, the one named last changes fastest.
Arguments:
- blocks: bfloat16 [2048, 8, 128, 128], P(('dom', 'col')), as said below
- a_cols: int32 [2048, 8], P('dom'), may hold values from -1 to 47, as said below
- near_null: bfloat16 [2048, 32, 128], P('dom'), may hold values from -6 to 6
- owner: int32 [2048], P('dom'), may hold values from 0 to 15
- p_mask: int32 [2048, 3, 16], P('dom', None, 'col'), may hold values 0 or 1
- ghost_send: int32 [64, 2, 8], P('dom'), may hold values from -1 to 31, as said below
Outputs:
- prolongator: bfloat16 [262144, 3, 512], P('dom', None, 'col')
Inputs may be any that keep to these rules, and one draw needn't show every extreme that they name: a_cols[r, 0] is r's own local index. Other entries: below 32 a block row of the same partition; 32 + s is slot s of ghost_send[d - 1, 1] of the partition before; 40 + s is slot s of ghost_send[d + 1, 0] of the partition after; -1 none. Referenced rows lie within 8 block rows of r, no column block is listed twice in a row, and every referenced slot holds a row. ghost_send[d, 0] lists, in slot order and packed at the front, block rows among the first 8 of partition d that partition d - 1 references; ghost_send[d, 1] those among the last 8 that partition d + 1 references; -1 fills empty slots; some partition fills all 8 slots. blocks[r, 0] has every diagonal entry at 0.5 or more.
All inputs are finite; a program needn't handle non-finite values. No bound on the sum of `p_mask` on one device may be relied on, other than what follows from the above.
Results may differ from a plain program's by a relative error of at most 0.0052.
Values may be sent and summed in bfloat16 or wider, within the bound.
A program may use at most 128 MiB of HBM per device.

v0:
```python
import jax
import jax.numpy as jnp
from jax import lax
from jax.sharding import PartitionSpec as P

SWEEPS = 3


OMEGA = 2.0 / 3.0
group_rows = 4


def shifted(shard, axis, by):
    length = lax.axis_size(axis)
    pairs = [(i, i + by) for i in range(length) if 0 <= i + by < length]
    return lax.ppermute(shard, axis, pairs)


def for_sending(shard):

    def short(part):
        return part.astype(jnp.bfloat16) if part.dtype == jnp.float32 else part

    return jax.tree.map(short, shard)


def pick_rows(source, row_list):
    picked = jnp.take(source, jnp.clip(row_list, 0, source.shape[0] - 1), axis=0)
    return jnp.where((row_list >= 0)[:, None, None, None], picked, jnp.zeros_like(picked))


def per_device(blocks, a_cols, near_null, owner, p_mask, ghost_send):
    full_blocks = lax.all_gather(blocks, "col", axis=0, tiled=True)
    block_rows = a_cols.shape[0]
    block_size = full_blocks.shape[2]
    slots = full_blocks.shape[1]
    local_aggs = p_mask.shape[2]
    vector_count = near_null.shape[1]
    ghost_count = ghost_send.shape[2]
    band_start = block_rows - ghost_count
    local_width = local_aggs * vector_count
    inverse_diag = 1.0 / jnp.diagonal(full_blocks[:, 0].astype(jnp.float32), axis1=1, axis2=2)
    aggregate_ids = lax.axis_index("col") * local_aggs + jnp.arange(local_aggs, dtype=jnp.int32)
    onehot = (owner[:, None] == aggregate_ids[None, :]).astype(jnp.bfloat16)
    vectors = jnp.transpose(near_null, (0, 2, 1))
    owned = (vectors[:, :, None, :] * onehot[:, None, :, None]).reshape(
        block_rows, block_size, local_width
    )
    empty = jnp.zeros_like(owned)
    prolong = jnp.stack([empty, owned, empty], axis=2)
    middle = (jnp.arange(3) == 1)[None, :, None]
    allowed = (p_mask > 0) | middle & (owner[:, None, None] == aggregate_ids[None, None, :])
    pattern = jnp.repeat(allowed, vector_count, axis=2)[:, None]
    column_index = jnp.where(a_cols < 0, block_rows + 2 * ghost_count, a_cols)
    groups = block_rows // group_rows
    grouped = (
        full_blocks.reshape((groups, group_rows) + full_blocks.shape[1:]),
        column_index.reshape(groups, group_rows, slots),
        inverse_diag.reshape(groups, group_rows, block_size),
        pattern.reshape((groups, group_rows) + pattern.shape[1:]),
    )
    lists_left = shifted(ghost_send, "dom", 1)
    lists_right = shifted(ghost_send, "dom", -1)
    left_rows = lists_left[0, 1]
    left_index = jnp.where(left_rows >= 0, left_rows - band_start, -1)
    right_index = lists_right[0, 0]
    for sweep_index in range(SWEEPS):
        band_left = shifted(for_sending(prolong[band_start:, :, 1:3]), "dom", 1)
        band_right = shifted(for_sending(prolong[:ghost_count, :, 0:2]), "dom", -1)
        left_in = pick_rows(band_left, left_index)
        right_in = pick_rows(band_right, right_index)
        empty_slot = jnp.zeros(left_in.shape[:2] + (1,) + left_in.shape[3:], jnp.bfloat16)
        extended = jnp.concatenate(
            [
                prolong,
                jnp.concatenate([left_in, empty_slot], axis=2),
                jnp.concatenate([empty_slot, right_in], axis=2),
                jnp.zeros((1,) + prolong.shape[1:], jnp.bfloat16),
            ],
            axis=0,
        )
        flat_extended = extended.reshape(extended.shape[0], block_size, 3 * local_width)

        def one_group(operands):
            group_blocks, group_cols, group_diag, group_pattern, group_p = operands
            total = jnp.zeros((group_rows, block_size, 3 * local_width), jnp.float32)
            for listed in range(slots):
                neighbour = jnp.take(flat_extended, group_cols[:, listed], axis=0)
                total = total + jnp.einsum(
                    "rij,rjx->rix",
                    group_blocks[:, listed],
                    neighbour,
                    preferred_element_type=jnp.float32,
                )
            total = total.reshape(group_rows, block_size, 3, local_width)
            updated = group_p.astype(jnp.float32) - OMEGA * group_diag[:, :, None, None] * total
            return jnp.where(group_pattern, updated, 0.0).astype(jnp.bfloat16)

        current = prolong.reshape((groups, group_rows) + prolong.shape[1:])
        prolong = lax.map(one_group, grouped + (current,)).reshape(prolong.shape)
    return prolong.reshape(block_rows * block_size, 3, local_width)


def solution(mesh):
    return jax.shard_map(
        per_device,
        mesh=mesh,
        in_specs=(
            P(("dom", "col"), None, None, None),
            P("dom", None),
            P("dom", None, None),
            P("dom"),
            P("dom", None, "col"),
            P("dom", None, None),
        ),
        out_specs=P("dom", None, "col"),
        check_vma=False,
    )
```

profile of v0, /device:TPU:97, one launch (start us, length us, event | category | flops | bytes accessed | tf_op | source)
XLA Modules:
  0.0 936.1 jit_solution(3633135219050081723)
XLA Ops:
  9.9 4.7 collective-permute-start
  20.0 4.9 collective-permute-start.1
  32.3 6.0 fusion.106
  38.4 4.1 copy.52
  42.4 7.5 copy.56
  49.9 46.8 %all-gather.2.cloned.1.call-done = bf16[32,8,128,128]{3,2,1,0:T(8,128)(2,1)} async-done(((bf16[8,8,128,128]{3,2,1,0:T(8,128)(2,1)}), bf16[32,8,128,128]{3,2,1,0:T(8,128)(2,1)}) %all-gather.2.cloned.1.call-update) | async-done | bytes 8388624 | tf_op jit(solution)/shard_map/all_gather | solution.py:33
  98.0 3.4 copy.67
  101.5 6.5 bitcast_convert_fusion
  109.8 10.4 %copy.55 = bf16[8,4,8,128,128]{4,3,1,2,0:T(8,128)(2,1)} copy(bf16[8,4,8,128,128]{4,3,2,1,0:T(8,128)(2,1)} %bitcast.219) | data formatting | bytes 16777216 | tf_op jit(solution)/shard_map/while | solution.py:100
  122.6 247.4 %while.30 = (s32[]{:T(128)}, bf16[8,4,128,3,128]{2,4,3,1,0:T(8,128)(2,1)}, pred[8,4,1,3,128]{4,3,1,2,0:T(4,128)(4,1)S(1)}, bf16[8,4,128,3,128]{2,4,1,0,3:T(8,128...) while((s32[]{:T(128)}, ...), condition=%wide.region_1.4_spmd, body=%wide.region_0.3_spmd.sunk | while | flops 406594304 | bytes 27575052 | solution.py:100
  127.6 3.0 gather_fusion.1
  134.4 3.0 gather_fusion.3
  137.8 3.0 gather_fusion.4
  144.5 3.0 gather_fusion.6
  147.9 3.0 gather_fusion.7
  158.6 3.0 gather_fusion.1
  165.3 3.0 gather_fusion.3
  168.7 3.0 gather_fusion.4
  172.0 3.0 gather_fusion.5
  175.4 3.0 gather_fusion.6
  178.8 3.0 gather_fusion.7
  371.3 4.9 collective-permute-start.4
  378.3 4.0 collective-permute-done.4
  383.1 4.8 collective-permute-done.5
  388.9 4.9 maximum_maximum_fusion
  393.8 7.5 copy.59
  403.7 247.4 %while.31 = (s32[]{:T(128)}, bf16[8,4,128,3,128]{2,4,3,1,0:T(8,128)(2,1)}, pred[8,4,1,3,128]{4,3,1,2,0:T(4,128)(4,1)S(1)}, bf16[8,4,128,3,128]{2,4,3,1,0:T(8,128...) while((s32[]{:T(128)}, ...), condition=%wide.region_3.6_spmd, body=%wide.region_2.5_spmd.sunk | while | flops 406594304 | bytes 27574540 | solution.py:100
  656.8 3.7 collective-permute-done.6
  661.3 4.8 collective-permute-done.7
  667.1 4.9 maximum_maximum_fusion.1
  672.0 7.5 copy.62
  679.4 249.9 %while.32 = (s32[]{:T(128)}, bf16[8,4,128,3,128]{4,2,1,0,3:T(8,128)(2,1)}, pred[8,4,1,3,128]{4,3,1,2,0:T(4,128)(4,1)S(1)}, bf16[8,4,128,3,128]{2,4,3,1,0:T(8,128...) while((s32[]{:T(128)}, ...), condition=%wide.region_5.8_spmd, body=%wide.region_4.7_spmd.sunk | while | flops 406594304 | bytes 29147408 | solution.py:100
  (1011 shorter events, 741.4 us)
Async XLA Ops:
  6.5 19.1 %copy-start = (bf16[32,32,128]{2,1,0:T(8,128)(2,1)S(1)}, bf16[32,32,128]{2,1,0:T(8,128)(2,1)}, u32[]{:S(2)}) copy-start(bf16[32,32,128]{2,1,0:T(8,128)(2,1)} %param.18) | copy-start | bytes 786436
  6.5 18.4 %copy-start.1 = (s32[32,3,4]{0,2,1:T(4,128)S(1)}, s32[32,3,4]{0,2,1:T(4,128)}, u32[]{:S(2)}) copy-start(s32[32,3,4]{0,2,1:T(4,128)} %param.20) | copy-start | bytes 4612
  6.5 19.0 %copy-start.2 = (s32[32,8]{0,1:T(8,128)S(1)}, s32[32,8]{0,1:T(8,128)}, u32[]{:S(2)}) copy-start(s32[32,8]{0,1:T(8,128)} %param.17) | copy-start | bytes 3076
  6.5 90.2 %all-gather.2.cloned.1.call-start = ((), (), s32[]{:S(2)}) async-start(), calls=%async_computation | async-start | bytes 10485760 | tf_op jit(solution)/shard_map/all_gather | solution.py:33
  7.3 21.5 %collective-permute-start.2 = (s32[1,2,8]{2,1,0:T(2,128)}, s32[1,2,8]{2,1,0:T(2,128)S(1)}, u32[]{:S(2)}, u32[]{:S(2)}) collective-permute-start(s32[1,2,8]{2,1,0:T(2,128)} %param.21), channel_id=1, source_target_pairs={{4,0},{8,4},{12,8},{16,12},{20,16},{24,20},{28,24},{32,28},{36,32}... | collective-permute-start | bytes 200 | tf_op jit(solution)/shard_map/ppermute | solution.py:16
  9.9 19.0 %collective-permute-start = (s32[1,2,8]{2,1,0:T(2,128)}, s32[1,2,8]{2,1,0:T(2,128)S(1)}, u32[]{:S(2)}, u32[]{:S(2)}) collective-permute-start(s32[1,2,8]{2,1,0:T(2,128)} %param.21), channel_id=1, source_target_pairs={{0,4},{4,8},{8,12},{12,16},{16,20},{20,24},{24,28},{28,32},{32,36}... | collective-permute-start | bytes 200 | tf_op jit(solution)/shard_map/ppermute | solution.py:16
  18.1 12.1 %collective-permute-start.3 = (bf16[8,128,2,128]{1,3,0,2:T(8,128)(2,1)S(1)}, bf16[8,128,2,128]{1,3,0,2:T(8,128)(2,1)S(1)}, u32[]{:S(2)}, u32[]{:S(2)}) collective-permute-start(bf16[8,128,2,128]{1,3,0,2:T(8,128)(2,1)S(1)} %get-tuple-element.339), channel_id=1, source_target_pairs={{4,0},{8,4},{12,8},{16,12},{20,16},{24,20},{28,24},{32,28},{36,32}... | collective-permute-start | bytes 1572872 | tf_op jit(solution)/shard_map/ppermute | solution.py:16
  20.0 11.3 %collective-permute-start.1 = (bf16[8,128,2,128]{1,3,0,2:T(8,128)(2,1)}, bf16[8,128,2,128]{1,3,0,2:T(8,128)(2,1)S(1)}, u32[]{:S(2)}, u32[]{:S(2)}) collective-permute-start(bf16[8,128,2,128]{1,3,0,2:T(8,128)(2,1)} %get-tuple-element.338), channel_id=1, source_target_pairs={{0,4},{4,8},{8,12},{12,16},{16,20},{20,24},{24,28},{28,32},{32,36}... | collective-permute-start | bytes 1572872 | tf_op jit(solution)/shard_map/ppermute | solution.py:16
  371.3 11.1 %collective-permute-start.4 = (bf16[8,128,2,128]{1,3,2,0:T(8,128)(2,1)S(1)}, bf16[8,128,2,128]{1,3,2,0:T(8,128)(2,1)S(1)}, u32[]{:S(2)}, u32[]{:S(2)}) collective-permute-start(bf16[8,128,2,128]{1,3,2,0:T(8,128)(2,1)S(1)} %get-tuple-element.336), channel_id=1, source_target_pairs={{0,4},{4,8},{8,12},{12,16},{16,20},{20,24},{24,28},{28,32},{32,36}... | collective-permute-start | bytes 1572872 | tf_op jit(solution)/shard_map/ppermute | solution.py:16
  376.2 11.7 %collective-permute-start.5 = (bf16[8,128,2,128]{1,3,2,0:T(8,128)(2,1)S(1)}, bf16[8,128,2,128]{1,3,2,0:T(8,128)(2,1)S(1)}, u32[]{:S(2)}, u32[]{:S(2)}) collective-permute-start(bf16[8,128,2,128]{1,3,2,0:T(8,128)(2,1)S(1)} %get-tuple-element.337), channel_id=1, source_target_pairs={{4,0},{8,4},{12,8},{16,12},{20,16},{24,20},{28,24},{32,28},{36,32}... | collective-permute-start | bytes 1572872 | tf_op jit(solution)/shard_map/ppermute | solution.py:16
  652.4 8.0 collective-permute-start.6
  654.4 11.7 %collective-permute-start.7 = (bf16[8,128,2,128]{1,3,2,0:T(8,128)(2,1)S(1)}, bf16[8,128,2,128]{1,3,2,0:T(8,128)(2,1)S(1)}, u32[]{:S(2)}, u32[]{:S(2)}) collective-permute-start(bf16[8,128,2,128]{1,3,2,0:T(8,128)(2,1)S(1)} %get-tuple-element.335), channel_id=1, source_target_pairs={{4,0},{8,4},{12,8},{16,12},{20,16},{24,20},{28,24},{32,28},{36,32}... | collective-permute-start | bytes 1572872 | tf_op jit(solution)/shard_map/ppermute | solution.py:16
Sparse Core Ops, SparseCore 0:
  9.2 87.5 all-gather.1
where the time goes:
time: 946 us; the launch traced here: 936 us
  local copies, waits for them, and re-layouts  686 us (73%)
  other arithmetic  73.6 us (8%)
  waiting for transfers between devices  66.5 us (7%)
  matrix products  64.1 us (7%)
  starting transfers between devices  25.4 us (3%)
  between operations  13.8 us (1%)
    gather x192, local copies, waits for them, and re-layouts, one_group(): neighbour = jnp.take(flat_extended, group_cols[:, listed], axis=0)  575 us
    dot_general x192, matrix products, one_group(): jnp.einsum('rij,rjx->rix', group_blocks[:, listed], neighbour, preferred_...  64.1 us
    all_gather x1, waiting for transfers between devices, per_device(): full_blocks = lax.all_gather(blocks, 'col', axis=0, tiled=True)  46.8 us
    while x5, local copies, waits for them, and re-layouts, per_device(): prolong = lax.map(one_group, grouped + (current,)).reshape(prolong.shape)  32.8 us
    dynamic_update_slice x16, other arithmetic, per_device(): prolong = lax.map(one_group, grouped + (current,)).reshape(prolong.shape)  32.5 us
    squeeze x48, local copies, waits for them, and re-layouts, per_device(): prolong = lax.map(one_group, grouped + (current,)).reshape(prolong.shape)  31.2 us
    ppermute x8, starting transfers between devices, shifted(): return lax.ppermute(shard, axis, pairs)  25.4 us
    ppermute x8, waiting for transfers between devices, shifted(): return lax.ppermute(shard, axis, pairs)  19 us
  transfers between devices with their start and end apart: 9, of which 7 were waited for; matrix products, arithmetic and copies ran while one was open for 3% of the time, Pallas kernels for 0%

commit v1 on v0

v1 whole, which is shorter than its diff:
```python
import jax
import jax.numpy as jnp
from jax import lax
from jax.experimental import pallas as pl
from jax.experimental.pallas import tpu as pltpu
from jax.sharding import PartitionSpec as P

OMEGA = 2.0 / 3.0
ROWS = 32
LISTED = 8
BLK = 128
COL = 4
GROUP = ROWS // COL
WIDTH = 2 * BLK
EMPTY = ROWS + 2 * GROUP
SLOTS = 12
AHEAD = 3
MESH = pl.DeviceIdType.MESH


def sent_row(group, position, leftward):
    first = 2 * position if not leftward else 2 * position + 1
    second = 2 * position - 7 if not leftward else 2 * position - 8
    place = jnp.where(position < 4, first, second)
    return group * GROUP + jnp.where(group < 2, place, GROUP - 1 - place)


def slot_row(sender, slot, leftward):
    forwards = (slot >= 3) & (slot <= 9) & (slot % 2 == 1)
    own = jnp.where(slot < 3, slot, jnp.where(slot == 11, 7, slot // 2 + 1))
    source = lax.rem(sender + jnp.where(leftward, 1, COL - 1), COL)
    group = jnp.where(forwards, source, sender)
    position = jnp.where(forwards, (slot - 3) // 2, own)
    return sent_row(group, position, leftward)


def kernel(
    cols, owner, mask_in, lists, blocks, vectors, out,
    held, p0, p1, p2, land0, land1, land2, scale, allow, stage, list_l, list_r, index_a, index_x, index_y,
    own_sem, send_sem, recv_sem, list_send, list_recv, ghost_send, ghost_recv, out_sem,
):
    pl.run_scoped(
        lambda *acc: body(
            cols, owner, mask_in, lists, blocks, vectors, out,
            held, p0, p1, p2, land0, land1, land2, scale, allow, stage, list_l, list_r, index_a, index_x, index_y,
            own_sem, send_sem, recv_sem, list_send, list_recv, ghost_send, ghost_recv, out_sem, acc,
        ),
        *[pltpu.ACC(mxu)((BLK, WIDTH), jnp.float32) for _ in range(2) for mxu in range(2)],
    )


def body(
    cols, owner, mask_in, lists, blocks, vectors, out,
    held, p0, p1, p2, land0, land1, land2, scale, allow, stage, list_l, list_r, index_a, index_x, index_y,
    own_sem, send_sem, recv_sem, list_send, list_recv, ghost_send, ghost_recv, out_sem, acc,
):
    me = lax.axis_index("col")
    part = lax.axis_index("dom")
    parts = lax.axis_size("dom")
    right, left = lax.rem(me + 1, COL), lax.rem(me + COL - 1, COL)
    after, before = lax.rem(part + 1, parts), lax.rem(part + parts - 1, parts)

    barrier = pltpu.get_barrier_semaphore()
    for axis, other in (("col", left), ("col", right), ("dom", before), ("dom", after)):
        pl.semaphore_signal(barrier, inc=1, device_id={axis: other}, device_id_type=MESH)
    pl.semaphore_wait(barrier, 4)

    own_copy = pltpu.make_async_copy(blocks, held.at[pl.ds(me * GROUP, GROUP)], own_sem)

    def gather_copy(slot, leftward, own):
        row = slot_row(me, slot, leftward)
        sem = (1 if leftward else 0), slot
        return pltpu.make_async_remote_copy(
            src_ref=blocks.at[row - me * GROUP] if own else held.at[row],
            dst_ref=held.at[row],
            send_sem=send_sem.at[sem],
            recv_sem=recv_sem.at[sem],
            device_id={"col": left if leftward else right},
            device_id_type=MESH,
        )

    def arrival(slot, leftward):
        row = slot_row(right if leftward else left, slot, leftward)
        sem = (1 if leftward else 0), slot
        return row, pltpu.make_async_remote_copy(
            src_ref=held.at[row],
            dst_ref=held.at[row],
            send_sem=send_sem.at[sem],
            recv_sem=recv_sem.at[sem],
            device_id={"col": left if leftward else right},
            device_id_type=MESH,
        )

    for slot in range(AHEAD):
        for leftward in (False, True):
            gather_copy(slot, leftward, True).start()
    own_copy.start()

    def list_copy(here, index, other):
        return pltpu.make_async_remote_copy(
            src_ref=lists,
            dst_ref=here,
            send_sem=list_send.at[index],
            recv_sem=list_recv.at[index],
            device_id={"dom": other},
            device_id_type=MESH,
        )

    list_copy(list_l, 0, after).start()
    list_copy(list_r, 1, before).start()

    def ghost_copy(source, target, sweep, row, place, count, other):
        src = source.at[pl.ds(row, count)] if count > 1 else source.at[row]
        dst = target.at[pl.ds(place, count)] if count > 1 else target.at[place]
        return pltpu.make_async_remote_copy(
            src_ref=src,
            dst_ref=dst,
            send_sem=ghost_send.at[sweep, place],
            recv_sem=ghost_recv.at[sweep, place],
            device_id={"dom": other},
            device_id_type=MESH,
        )

    @pl.loop(0, ROWS)
    def _(r):
        values = vectors[r].astype(jnp.float32)
        tall = jnp.concatenate([values] * 4, axis=0)
        aggregate = lax.broadcasted_iota(jnp.int32, (BLK, BLK), 0) // 32 + me * 4
        owned = jnp.where(aggregate == owner[r], tall, 0.0)
        middle = jnp.transpose(owned).astype(jnp.bfloat16)
        p0[r] = jnp.concatenate([jnp.zeros((BLK, BLK), jnp.bfloat16), middle], axis=1)

    ghost_copy(p0, land0, 0, 0, GROUP, GROUP, before).start()
    ghost_copy(p0, land0, 0, ROWS - GROUP, 0, GROUP, after).start()
    for buffer in (p0, p1, p2):
        buffer[EMPTY] = jnp.zeros((BLK, WIDTH), jnp.bfloat16)
    nothing = jnp.zeros((GROUP * BLK, BLK), jnp.bfloat16)
    stage[2, 0 : GROUP * BLK, :] = nothing
    stage[0, (ROWS - GROUP) * BLK : ROWS * BLK, :] = nothing

    lane = lax.broadcasted_iota(jnp.int32, (1, BLK), 1) // 32
    for half, order in ((0, (0, 1, 2)), (1, (2, 1, 0))):
        @pl.loop(half * ROWS // 2, (half + 1) * ROWS // 2)
        def _(r):
            pieces = []
            for w in order:
                piece = jnp.zeros((1, BLK), jnp.int32)
                for a in range(4):
                    value = mask_in[w, a, r]
                    if w == 1:
                        value = jnp.where(owner[r] == me * 4 + a, 1, value)
                    piece = jnp.where(lane == a, value, piece)
                pieces.append(piece)
            allow[r] = jnp.concatenate(pieces, axis=1)

    list_copy(list_l, 0, after).wait()
    list_copy(list_r, 1, before).wait()

    @pl.loop(0, ROWS)
    def _(r):
        for k in range(LISTED):
            c = cols[k, r]
            from_left = list_l[0, 1, jnp.clip(c - ROWS, 0, GROUP - 1)] - (ROWS - GROUP)
            from_right = list_r[0, 0, jnp.clip(c - ROWS - GROUP, 0, GROUP - 1)]
            from_left = jnp.where(from_left < 0, EMPTY, from_left + ROWS)
            from_right = jnp.where(from_right < 0, EMPTY, from_right + ROWS + GROUP)
            place = jnp.where(c < ROWS, c, jnp.where(c < ROWS + GROUP, from_left, from_right))
            place = jnp.where(c < 0, EMPTY, place)
            lower = (place < ROWS // 2) | ((place >= ROWS) & (place < ROWS + GROUP))
            index_a[r * LISTED + k] = place
            index_x[r * LISTED + k] = jnp.where(lower, place, EMPTY)
            index_y[r * LISTED + k] = jnp.where(lower, EMPTY, place)

    def settle(target, landed, place):
        value = landed[place]
        value = jnp.concatenate([value[:, BLK:], value[:, :BLK]], axis=1)
        exists = jnp.where(place < GROUP, part > 0, part < parts - 1)
        target[ROWS + place] = jnp.where(exists, value, jnp.zeros_like(value))

    ghost_copy(p0, land0, 0, 0, GROUP, GROUP, before).wait()
    ghost_copy(p0, land0, 0, ROWS - GROUP, 0, GROUP, after).wait()

    @pl.loop(0, 2 * GROUP)
    def _(place):
        settle(p0, land0, place)

    def issue(source, index, r, bank, mxu, q):
        def tile(k):
            return source[index[r * LISTED + k]]

        pltpu.matmul_push_rhs(jnp.concatenate([tile(2 * q), tile(2 * q + 1)], axis=0), q % 2, mxu)

    def multiply(r, bank, mxu, q):
        lhs = jnp.concatenate([held[r, 2 * q], held[r, 2 * q + 1]], axis=1)
        pltpu.matmul_acc_lhs(acc[2 * bank + mxu], lhs, load_staged_rhs=q % 2)

    def product(source, work, bank):
        for q in range(LISTED // 2):
            for mxu, (r, index) in enumerate(work):
                issue(source, index, r, bank, mxu, q)
            for mxu, (r, index) in enumerate(work):
                multiply(r, bank, mxu, q)

    def update(source, r, total):
        factor = scale[r]
        value = source[r].astype(jnp.float32) - jnp.concatenate([factor, factor], axis=1) * total
        return jnp.where(allow[r][:, :WIDTH] > 0, value, 0.0).astype(jnp.bfloat16)

    def make_scale(r):
        diagonal = lax.broadcasted_iota(jnp.int32, (BLK, BLK), 0) == lax.broadcasted_iota(jnp.int32, (BLK, BLK), 1)
        entries = jnp.sum(jnp.where(diagonal, held[r, 0].astype(jnp.float32), 0.0), axis=1, keepdims=True)
        scale[r] = jnp.broadcast_to(OMEGA * (1.0 / entries), (BLK, BLK))

    def sweep_rows(source, target, rows, after_row=None):
        pairs = [rows[i : i + 2] for i in range(0, len(rows), 2)]

        def finish(number):
            for mxu, r in enumerate(pairs[number]):
                target[r] = update(source, r, pltpu.matmul_pop(acc[2 * (number % 2) + mxu]))
                if after_row is not None:
                    after_row(r)

        for number, pair in enumerate(pairs):
            product(source, [(r, index_a) for r in pair], number % 2)
            if number > 0:
                finish(number - 1)
        finish(len(pairs) - 1)

    def send_ghost(source, landed, sweep):
        def start(r):
            @pl.when(r < GROUP)
            def _():
                ghost_copy(source, landed, sweep, r, GROUP + r, 1, before).start()

            @pl.when(r >= ROWS - GROUP)
            def _():
                ghost_copy(source, landed, sweep, r, r - (ROWS - GROUP), 1, after).start()

        return start

    own_copy.wait()

    @pl.loop(0, GROUP)
    def _(i):
        make_scale(me * GROUP + i)

    sweep_rows(p0, p1, [me * GROUP + i for i in range(GROUP)], send_ghost(p1, land1, 1))

    @pl.loop(0, SLOTS)
    def _(slot):
        row_l, copy_l = arrival(slot, False)
        row_r, copy_r = arrival(slot, True)
        copy_l.wait_recv()
        copy_r.wait_recv()
        later = slot + AHEAD
        forwards = (later <= 9) & (later % 2 == 1)

        @pl.when(forwards)
        def _():
            gather_copy(later, False, False).start()
            gather_copy(later, True, False).start()

        @pl.when((later < SLOTS) & jnp.logical_not(forwards))
        def _():
            gather_copy(later, False, True).start()
            gather_copy(later, True, True).start()

        make_scale(row_l)
        make_scale(row_r)
        sweep_rows(p0, p1, [row_l, row_r], send_ghost(p1, land1, 1))

    def settle_all(source, target, landed, sweep):
        @pl.loop(0, GROUP)
        def _(i):
            ghost_copy(source, landed, sweep, i, GROUP + i, 1, before).wait_recv()
            settle(target, landed, GROUP + i)
            ghost_copy(source, landed, sweep, ROWS - GROUP + i, i, 1, after).wait_recv()
            settle(target, landed, i)

    @pl.loop(GROUP, ROWS - GROUP, step=8)
    def _(r):
        sweep_rows(p1, p2, [r + i for i in range(8)])

    settle_all(p1, p1, land1, 1)

    @pl.loop(0, 2)
    def _(half):
        base = half * (ROWS - GROUP)
        sweep_rows(p1, p2, [base + i for i in range(8)], send_ghost(p2, land2, 2))

    def out_copy(w, r, count):
        place = pl.ds(pl.multiple_of(r * BLK, BLK), count * BLK)
        return pltpu.make_async_copy(stage.at[w, place], out.at[w, place], out_sem.at[w])

    def put(w, r, value):
        stage[w, pl.ds(pl.multiple_of(r * BLK, BLK), BLK), :] = value

    def inner_rows(rows, upper):
        near, far = (2, 0) if upper else (0, 2)

        def finish(number):
            r = rows[number]
            lower_sum = pltpu.matmul_pop(acc[2 * (number % 2)])
            upper_sum = pltpu.matmul_pop(acc[2 * (number % 2) + 1])
            middle = lower_sum[:, BLK:] + upper_sum[:, BLK:]
            near_sum, far_sum = (upper_sum, lower_sum) if upper else (lower_sum, upper_sum)
            factor = scale[r]
            old = p2[r].astype(jnp.float32)
            mask = allow[r]
            put(near, r, jnp.where(mask[:, :BLK] > 0, old[:, :BLK] - factor * near_sum[:, :BLK], 0.0).astype(jnp.bfloat16))
            put(1, r, jnp.where(mask[:, BLK:WIDTH] > 0, old[:, BLK:] - factor * middle, 0.0).astype(jnp.bfloat16))
            put(far, r, jnp.where(mask[:, WIDTH:] > 0, 0.0 - factor * far_sum[:, :BLK], 0.0).astype(jnp.bfloat16))

        for number, r in enumerate(rows):
            product(p2, [(r, index_x), (r, index_y)], number % 2)
            if number > 0:
                finish(number - 1)
        finish(len(rows) - 1)

    for upper in (False, True):
        @pl.loop(ROWS // 2 - GROUP + upper * GROUP, ROWS // 2 + upper * GROUP, step=4)
        def _(r):
            inner_rows([r + i for i in range(4)], upper)

    settle_all(p2, p2, land2, 2)

    def outer_rows(rows, outer):
        pairs = [rows[i : i + 2] for i in range(0, len(rows), 2)]

        def finish(number):
            for mxu, r in enumerate(pairs[number]):
                value = update(p2, r, pltpu.matmul_pop(acc[2 * (number % 2) + mxu]))
                put(outer, r, value[:, :BLK])
                put(1, r, value[:, BLK:])

        for number, pair in enumerate(pairs):
            product(p2, [(r, index_a) for r in pair], number % 2)
            if number > 0:
                finish(number - 1)
        finish(len(pairs) - 1)

    outer_rows([i for i in range(GROUP)], 0)
    outer_rows([ROWS - GROUP + i for i in range(GROUP)], 2)
    for w in range(3):
        out_copy(w, 0, ROWS).start()

    @pl.loop(0, SLOTS)
    def _(slot):
        forwards = (slot >= 3) & (slot <= 9) & (slot % 2 == 1)

        @pl.when(forwards)
        def _():
            gather_copy(slot, False, False).wait_send()
            gather_copy(slot, True, False).wait_send()

        @pl.when(jnp.logical_not(forwards))
        def _():
            gather_copy(slot, False, True).wait_send()
            gather_copy(slot, True, True).wait_send()

    @pl.loop(0, GROUP)
    def _(i):
        for source, landed, sweep in ((p1, land1, 1), (p2, land2, 2)):
            ghost_copy(source, landed, sweep, i, GROUP + i, 1, before).wait_send()
            ghost_copy(source, landed, sweep, ROWS - GROUP + i, i, 1, after).wait_send()

    for w in range(3):
        out_copy(w, 0, ROWS).wait()


def per_device(blocks, a_cols, near_null, owner, p_mask, ghost_send):
    scalar = pl.BlockSpec(memory_space=pltpu.SMEM)
    anywhere = pl.BlockSpec(memory_space=pl.ANY)
    dma = pltpu.SemaphoreType.DMA
    kept = pltpu.VMEM((EMPTY + 1, BLK, WIDTH), jnp.bfloat16)
    landing = pltpu.VMEM((2 * GROUP, BLK, WIDTH), jnp.bfloat16)
    index = pltpu.SMEM((ROWS * LISTED,), jnp.int32)
    result = pl.pallas_call(
        kernel,
        out_shape=jax.ShapeDtypeStruct((3, ROWS * BLK, BLK), jnp.bfloat16),
        in_specs=[scalar, scalar, scalar, anywhere, anywhere, pl.BlockSpec(memory_space=pltpu.VMEM)],
        out_specs=anywhere,
        scratch_shapes=[
            pltpu.VMEM((ROWS, LISTED, BLK, BLK), jnp.bfloat16),
            kept,
            kept,
            kept,
            landing,
            landing,
            landing,
            pltpu.VMEM((ROWS, BLK, BLK), jnp.float32),
            pltpu.VMEM((ROWS, 1, 3 * BLK), jnp.int32),
            pltpu.VMEM((3, ROWS * BLK, BLK), jnp.bfloat16),
            pltpu.SMEM((1, 2, GROUP), jnp.int32),
            pltpu.SMEM((1, 2, GROUP), jnp.int32),
            index,
            index,
            index,
            dma,
            dma((2, SLOTS)),
            dma((2, SLOTS)),
            dma((2,)),
            dma((2,)),
            dma((3, 2 * GROUP)),
            dma((3, 2 * GROUP)),
            dma((3,)),
        ],
        compiler_params=pltpu.CompilerParams(collective_id=0, has_side_effects=True, vmem_limit_bytes=48 << 20),
        cost_estimate=pl.CostEstimate(flops=10_000_000_000, bytes_accessed=16_000_000, transcendentals=0),
    )(a_cols.T, owner, p_mask.transpose(1, 2, 0), ghost_send, blocks, near_null)
    return result.transpose(1, 0, 2)


def solution(mesh):
    return jax.shard_map(
        per_device,
        mesh=mesh,
        in_specs=(
            P(("dom", "col"), None, None, None),
            P("dom", None),
            P("dom", None, None),
            P("dom"),
            P("dom", None, "col"),
            P("dom", None, None),
        ),
        out_specs=P("dom", None, "col"),
        check_vma=False,
    )
```

time: 946 us -> 99.6 us (0.11)
  the two profiles are of different devices: /device:TPU:97 before, /device:TPU:2 now
where the time goes in v1:
time: 99.6 us; the launch traced here: 99.3 us
  Pallas kernels  92.4 us (93%)
  local copies, waits for them, and re-layouts  6.92 us (7%)
    pallas_call x1, Pallas kernels, per_device(): pl.pallas_call(kernel, out_shape=jax.ShapeDtypeStruct((3, ROWS * BLK, BLK...  92.4 us
    unnamed x13, local copies, waits for them, and re-layouts  6.92 us

profile of v1, /device:TPU:2, one launch (start us, length us, event | category | flops | bytes accessed | tf_op | source)
XLA Modules:
  0.0 99.3 jit_solution(13948397961135939703)
XLA Ops:
  0.0 0.0 copy-start
  0.0 1.6 %copy-done = bf16[8,8,128,128]{3,2,1,0:T(8,128)(2,1)S(1)} copy-done((bf16[8,8,128,128]{3,2,1,0:T(8,128)(2,1)S(1)}, bf16[8,8,128,128]{3,2,1,0:T(8,128)(2,1)}, u32[]{:S(2)}) %copy-start) | copy-done | bytes 2097176
  1.6 0.0 copy-start.1
  1.6 0.9 copy-done.1
  2.5 0.0 copy-start.2
  2.5 0.7 copy-done.2
  3.2 0.0 copy-start.3
  3.2 0.7 copy-done.3
  3.9 0.0 copy-start.4
  3.9 0.7 copy-done.4
  4.6 0.0 copy-start.5
  4.6 0.7 copy-done.5
  5.3 92.4 %shard_map.64 = bf16[3,4096,128]{2,1,0:T(8,128)(2,1)S(1)} custom-call(s32[8,32]{1,0:T(8,128)S(1)} %bitcast.5, s32[32]{0:T(128)S(1)} %copy-done.5, s32[3,4,32]{2,1,0:T(4,128)S(1)} %bitcast.4, s32[1,2,8]{2,1,0:T(2,128)S(1)} %copy-done.4, bf16[8,8,128,128]{3,2,1,0:T(8,128)(2,1)S(1)} %copy-done, bf16[32,32,128]{2,1,0:T(8,128)(2,1)S(1)} %copy-done.1), custom_call_target="tpu_custom_call" | custom-call | flops 10000000000 | bytes 16000000 | tf_op jit(solution)/shard_map/pallas_call | solution.py:378
  97.7 1.7 %copy.8 = bf16[4096,3,128]{2,0,1:T(8,128)(2,1)} copy(bf16[4096,3,128]{2,0,1:T(8,128)(2,1)S(1)} %bitcast.3) | data formatting | bytes 6291456
Async XLA Ops:
  0.0 1.6 %copy-start = (bf16[8,8,128,128]{3,2,1,0:T(8,128)(2,1)S(1)}, bf16[8,8,128,128]{3,2,1,0:T(8,128)(2,1)}, u32[]{:S(2)}) copy-start(bf16[8,8,128,128]{3,2,1,0:T(8,128)(2,1)} %blocks.1) | copy-start | bytes 6291460
  1.6 0.9 copy-start.1
  2.5 0.7 copy-start.2
  3.2 0.7 copy-start.3
  3.9 0.7 copy-start.4
  4.6 0.7 copy-start.5

commit v2 on v1

--- a/solution.py
+++ b/solution.py
@@ -14,7 +14,6 @@
 WIDTH = 2 * BLK
 EMPTY = ROWS + 2 * GROUP
 SLOTS = 12
-AHEAD = 3
 MESH = pl.DeviceIdType.MESH
 
 
@@ -26,33 +25,32 @@
 
 
 def slot_row(sender, slot, leftward):
-    forwards = (slot >= 3) & (slot <= 9) & (slot % 2 == 1)
-    own = jnp.where(slot < 3, slot, jnp.where(slot == 11, 7, slot // 2 + 1))
+    forwards = slot >= GROUP
     source = lax.rem(sender + jnp.where(leftward, 1, COL - 1), COL)
     group = jnp.where(forwards, source, sender)
-    position = jnp.where(forwards, (slot - 3) // 2, own)
+    position = jnp.where(forwards, slot - GROUP, slot)
     return sent_row(group, position, leftward)
 
 
 def kernel(
-    cols, owner, mask_in, lists, blocks, vectors, out,
-    held, p0, p1, p2, land0, land1, land2, scale, allow, stage, list_l, list_r, index_a, index_x, index_y,
-    own_sem, send_sem, recv_sem, list_send, list_recv, ghost_send, ghost_recv, out_sem,
+    cols_in, owner_in, mask_at, lists, blocks, vectors_in, out,
+    cols, owner, mask_in, vectors, in_sem, held, p0, p1, p2, land0, land1, land2, scale, allow, partial, list_l, list_r, index_a, index_x, index_y, find_a, find_b,
+    own_sem, send_sem, recv_sem, list_send, list_recv, ghost_send, ghost_recv,
 ):
     pl.run_scoped(
         lambda *acc: body(
-            cols, owner, mask_in, lists, blocks, vectors, out,
-            held, p0, p1, p2, land0, land1, land2, scale, allow, stage, list_l, list_r, index_a, index_x, index_y,
-            own_sem, send_sem, recv_sem, list_send, list_recv, ghost_send, ghost_recv, out_sem, acc,
+            cols_in, owner_in, mask_at, lists, blocks, vectors_in, out,
+            cols, owner, mask_in, vectors, in_sem, held, p0, p1, p2, land0, land1, land2, scale, allow, partial, list_l, list_r, index_a, index_x, index_y, find_a, find_b,
+            own_sem, send_sem, recv_sem, list_send, list_recv, ghost_send, ghost_recv, acc,
         ),
         *[pltpu.ACC(mxu)((BLK, WIDTH), jnp.float32) for _ in range(2) for mxu in range(2)],
     )
 
 
 def body(
-    cols, owner, mask_in, lists, blocks, vectors, out,
-    held, p0, p1, p2, land0, land1, land2, scale, allow, stage, list_l, list_r, index_a, index_x, index_y,
-    own_sem, send_sem, recv_sem, list_send, list_recv, ghost_send, ghost_recv, out_sem, acc,
+    cols_in, owner_in, mask_at, lists, blocks, vectors_in, out,
+    cols, owner, mask_in, vectors, in_sem, held, p0, p1, p2, land0, land1, land2, scale, allow, partial, list_l, list_r, index_a, index_x, index_y, find_a, find_b,
+    own_sem, send_sem, recv_sem, list_send, list_recv, ghost_send, ghost_recv, acc,
 ):
     me = lax.axis_index("col")
     part = lax.axis_index("dom")
@@ -60,6 +58,14 @@
     right, left = lax.rem(me + 1, COL), lax.rem(me + COL - 1, COL)
     after, before = lax.rem(part + 1, parts), lax.rem(part + parts - 1, parts)
 
+    loads = [
+        pltpu.make_async_copy(source, target, in_sem.at[number])
+        for number, (source, target) in enumerate(
+            ((vectors_in, vectors), (owner_in, owner), (mask_at, mask_in), (cols_in, cols))
+        )
+    ]
+    for load in loads:
+        load.start()
     barrier = pltpu.get_barrier_semaphore()
     for axis, other in (("col", left), ("col", right), ("dom", before), ("dom", after)):
         pl.semaphore_signal(barrier, inc=1, device_id={axis: other}, device_id_type=MESH)
@@ -91,7 +97,7 @@
             device_id_type=MESH,
         )
 
-    for slot in range(AHEAD):
+    for slot in range(GROUP):
         for leftward in (False, True):
             gather_copy(slot, leftward, True).start()
     own_copy.start()
@@ -121,6 +127,9 @@
             device_id_type=MESH,
         )
 
+    for load in loads:
+        load.wait()
+
     @pl.loop(0, ROWS)
     def _(r):
         values = vectors[r].astype(jnp.float32)
@@ -134,9 +143,22 @@
     ghost_copy(p0, land0, 0, ROWS - GROUP, 0, GROUP, after).start()
     for buffer in (p0, p1, p2):
         buffer[EMPTY] = jnp.zeros((BLK, WIDTH), jnp.bfloat16)
+    held[ROWS, 0] = jnp.zeros((BLK, BLK), jnp.bfloat16)
     nothing = jnp.zeros((GROUP * BLK, BLK), jnp.bfloat16)
-    stage[2, 0 : GROUP * BLK, :] = nothing
-    stage[0, (ROWS - GROUP) * BLK : ROWS * BLK, :] = nothing
+    out[2, 0 : GROUP * BLK, :] = nothing
+    out[0, (ROWS - GROUP) * BLK : ROWS * BLK, :] = nothing
+
+    late_pair = sent_row(lax.rem(me + 2, COL), SLOTS - GROUP - 1, False) // 2
+    late_a, late_b = 2 * late_pair, 2 * late_pair + 1
+    edge_pair = jnp.where(me == 2, ROWS // 2 - 1, 0)
+
+    def other_pair(number, turn):
+        first = lax.rem(late_pair + turn, ROWS // 2)
+        second = lax.rem(edge_pair + turn, ROWS // 2)
+        low, high = jnp.minimum(first, second), jnp.maximum(first, second)
+        place = number + jnp.where(number >= low, 1, 0)
+        place = place + jnp.where(place >= high, 1, 0)
+        return lax.rem(place + ROWS // 2 - turn, ROWS // 2)
 
     lane = lax.broadcasted_iota(jnp.int32, (1, BLK), 1) // 32
     for half, order in ((0, (0, 1, 2)), (1, (2, 1, 0))):
@@ -158,6 +180,8 @@
 
     @pl.loop(0, ROWS)
     def _(r):
+        found_a = jnp.int32(LISTED)
+        found_b = jnp.int32(LISTED)
         for k in range(LISTED):
             c = cols[k, r]
             from_left = list_l[0, 1, jnp.clip(c - ROWS, 0, GROUP - 1)] - (ROWS - GROUP)
@@ -170,6 +194,10 @@
             index_a[r * LISTED + k] = place
             index_x[r * LISTED + k] = jnp.where(lower, place, EMPTY)
             index_y[r * LISTED + k] = jnp.where(lower, EMPTY, place)
+            found_a = jnp.where(place == late_a, k, found_a)
+            found_b = jnp.where(place == late_b, k, found_b)
+        find_a[r] = found_a
+        find_b[r] = found_b
 
     def settle(target, landed, place):
         value = landed[place]
@@ -217,14 +245,15 @@
         def finish(number):
             for mxu, r in enumerate(pairs[number]):
                 target[r] = update(source, r, pltpu.matmul_pop(acc[2 * (number % 2) + mxu]))
-                if after_row is not None:
-                    after_row(r)
 
         for number, pair in enumerate(pairs):
             product(source, [(r, index_a) for r in pair], number % 2)
             if number > 0:
                 finish(number - 1)
         finish(len(pairs) - 1)
+        if after_row is not None:
+            for r in rows:
+                after_row(r)
 
     def send_ghost(source, landed, sweep):
         def start(r):
@@ -246,54 +275,110 @@
 
     sweep_rows(p0, p1, [me * GROUP + i for i in range(GROUP)], send_ghost(p1, land1, 1))
 
-    @pl.loop(0, SLOTS)
-    def _(slot):
+    def receive(slot):
         row_l, copy_l = arrival(slot, False)
         row_r, copy_r = arrival(slot, True)
         copy_l.wait_recv()
         copy_r.wait_recv()
-        later = slot + AHEAD
-        forwards = (later <= 9) & (later % 2 == 1)
-
-        @pl.when(forwards)
-        def _():
-            gather_copy(later, False, False).start()
-            gather_copy(later, True, False).start()
-
-        @pl.when((later < SLOTS) & jnp.logical_not(forwards))
-        def _():
-            gather_copy(later, False, True).start()
-            gather_copy(later, True, True).start()
-
+        return row_l, row_r
+
+    def first_sweep(row_l, row_r):
         make_scale(row_l)
         make_scale(row_r)
         sweep_rows(p0, p1, [row_l, row_r], send_ghost(p1, land1, 1))
 
-    def settle_all(source, target, landed, sweep):
-        @pl.loop(0, GROUP)
-        def _(i):
-            ghost_copy(source, landed, sweep, i, GROUP + i, 1, before).wait_recv()
-            settle(target, landed, GROUP + i)
-            ghost_copy(source, landed, sweep, ROWS - GROUP + i, i, 1, after).wait_recv()
-            settle(target, landed, i)
-
-    @pl.loop(GROUP, ROWS - GROUP, step=8)
-    def _(r):
-        sweep_rows(p1, p2, [r + i for i in range(8)])
-
-    settle_all(p1, p1, land1, 1)
-
-    @pl.loop(0, 2)
-    def _(half):
-        base = half * (ROWS - GROUP)
-        sweep_rows(p1, p2, [base + i for i in range(8)], send_ghost(p2, land2, 2))
-
-    def out_copy(w, r, count):
-        place = pl.ds(pl.multiple_of(r * BLK, BLK), count * BLK)
-        return pltpu.make_async_copy(stage.at[w, place], out.at[w, place], out_sem.at[w])
+    p1[late_a] = jnp.zeros((BLK, WIDTH), jnp.bfloat16)
+    p1[late_b] = jnp.zeros((BLK, WIDTH), jnp.bfloat16)
+
+    @pl.loop(0, SLOTS - GROUP)
+    def _(slot):
+        rows = receive(slot)
+        gather_copy(slot + GROUP, False, False).start()
+        gather_copy(slot + GROUP, True, False).start()
+        first_sweep(*rows)
+
+    @pl.loop(SLOTS - GROUP, SLOTS - 1)
+    def _(slot):
+        first_sweep(*receive(slot))
+
+    def take_ghost(source, landed, sweep, place):
+        @pl.when(place < GROUP)
+        def _():
+            ghost_copy(source, landed, sweep, ROWS - GROUP + place, place, 1, after).wait_recv()
+
+        @pl.when(place >= GROUP)
+        def _():
+            ghost_copy(source, landed, sweep, place - GROUP, place, 1, before).wait_recv()
+
+        settle(source, landed, place)
+
+    def partial_rows(numbers):
+        pairs = [other_pair(number, ROWS // 2 - 4) for number in numbers]
+
+        def finish(number):
+            for mxu in range(2):
+                partial[2 * pairs[number] + mxu] = pltpu.matmul_pop(acc[2 * (number % 2) + mxu])
+
+        for number, pair in enumerate(pairs):
+            product(p1, [(2 * pair, index_a), (2 * pair + 1, index_a)], number % 2)
+            if number > 0:
+                finish(number - 1)
+        finish(len(pairs) - 1)
+
+    late_ghost = jnp.where(me == 2, 2 * GROUP - 2, 0)
+    p1[ROWS + late_ghost] = jnp.zeros((BLK, WIDTH), jnp.bfloat16)
+    p1[ROWS + late_ghost + 1] = jnp.zeros((BLK, WIDTH), jnp.bfloat16)
+    partial_rows(range(7))
+
+    @pl.loop(0, 2 * GROUP - 2)
+    def _(i):
+        take_ghost(p1, land1, 1, i + jnp.where(me == 2, 0, 2))
+
+    partial_rows(range(7, 14))
+    first_sweep(*receive(SLOTS - 1))
+
+    send_second = send_ghost(p2, land2, 2)
+    sweep_rows(p1, p2, [late_a, late_b], send_second)
+
+    def corrected_rows(numbers):
+        pairs = [other_pair(number, 4) for number in numbers]
+
+        def finish(number):
+            for mxu in range(2):
+                r = 2 * pairs[number] + mxu
+                total = partial[r] + pltpu.matmul_pop(acc[2 * (number % 2) + mxu])
+                p2[r] = update(p1, r, total)
+
+        tile = jnp.concatenate([p1[late_a], p1[late_b]], axis=0)
+        for mxu in range(2):
+            pltpu.matmul_push_rhs(tile, 0, mxu)
+        for number, pair in enumerate(pairs):
+            for mxu in range(2):
+                r = 2 * pair + mxu
+                k_a, k_b = find_a[r], find_b[r]
+                lhs = [held[jnp.where(k < LISTED, r, ROWS), jnp.where(k < LISTED, k, 0)] for k in (k_a, k_b)]
+                pltpu.matmul_acc_lhs(
+                    acc[2 * (number % 2) + mxu],
+                    jnp.concatenate(lhs, axis=1),
+                    load_staged_rhs=0 if number == 0 else None,
+                )
+            if number > 0:
+                finish(number - 1)
+        finish(len(pairs) - 1)
+        if numbers[0] < 7:
+            for pair in pairs:
+                send_second(2 * pair)
+                send_second(2 * pair + 1)
+
+    corrected_rows(range(4))
+    corrected_rows(range(4, 7))
+    corrected_rows(range(7, 14))
+    take_ghost(p1, land1, 1, late_ghost)
+    take_ghost(p1, land1, 1, late_ghost + 1)
+    sweep_rows(p1, p2, [2 * edge_pair, 2 * edge_pair + 1], send_second)
 
     def put(w, r, value):
-        stage[w, pl.ds(pl.multiple_of(r * BLK, BLK), BLK), :] = value
+        out[w, pl.ds(pl.multiple_of(r * BLK, BLK), BLK), :] = value
 
     def inner_rows(rows, upper):
         near, far = (2, 0) if upper else (0, 2)
@@ -322,8 +407,6 @@
         def _(r):
             inner_rows([r + i for i in range(4)], upper)
 
-    settle_all(p2, p2, land2, 2)
-
     def outer_rows(rows, outer):
         pairs = [rows[i : i + 2] for i in range(0, len(rows), 2)]
 
@@ -339,21 +422,24 @@
                 finish(number - 1)
         finish(len(pairs) - 1)
 
-    outer_rows([i for i in range(GROUP)], 0)
-    outer_rows([ROWS - GROUP + i for i in range(GROUP)], 2)
-    for w in range(3):
-        out_copy(w, 0, ROWS).start()
+    @pl.loop(0, 2)
+    def _(number):
+        upper = jnp.where(me == 2, number, 1 - number)
+
+        @pl.loop(0, GROUP)
+        def _(i):
+            take_ghost(p2, land2, 2, upper * GROUP + i)
+
+        outer_rows([upper * (ROWS - GROUP) + i for i in range(GROUP)], 2 * upper)
 
     @pl.loop(0, SLOTS)
     def _(slot):
-        forwards = (slot >= 3) & (slot <= 9) & (slot % 2 == 1)
-
-        @pl.when(forwards)
+        @pl.when(slot >= GROUP)
         def _():
             gather_copy(slot, False, False).wait_send()
             gather_copy(slot, True, False).wait_send()
 
-        @pl.when(jnp.logical_not(forwards))
+        @pl.when(slot < GROUP)
         def _():
             gather_copy(slot, False, True).wait_send()
             gather_copy(slot, True, True).wait_send()
@@ -364,24 +450,25 @@
             ghost_copy(source, landed, sweep, i, GROUP + i, 1, before).wait_send()
             ghost_copy(source, landed, sweep, ROWS - GROUP + i, i, 1, after).wait_send()
 
-    for w in range(3):
-        out_copy(w, 0, ROWS).wait()
-
 
 def per_device(blocks, a_cols, near_null, owner, p_mask, ghost_send):
-    scalar = pl.BlockSpec(memory_space=pltpu.SMEM)
-    anywhere = pl.BlockSpec(memory_space=pl.ANY)
+    hbm = pl.BlockSpec(memory_space=pltpu.HBM)
     dma = pltpu.SemaphoreType.DMA
     kept = pltpu.VMEM((EMPTY + 1, BLK, WIDTH), jnp.bfloat16)
     landing = pltpu.VMEM((2 * GROUP, BLK, WIDTH), jnp.bfloat16)
     index = pltpu.SMEM((ROWS * LISTED,), jnp.int32)
     result = pl.pallas_call(
         kernel,
-        out_shape=jax.ShapeDtypeStruct((3, ROWS * BLK, BLK), jnp.bfloat16),
-        in_specs=[scalar, scalar, scalar, anywhere, anywhere, pl.BlockSpec(memory_space=pltpu.VMEM)],
-        out_specs=anywhere,
+        out_shape=pltpu.VMEM((3, ROWS * BLK, BLK), jnp.bfloat16),
+        in_specs=[hbm] * 6,
+        out_specs=pl.BlockSpec(memory_space=pltpu.VMEM),
         scratch_shapes=[
-            pltpu.VMEM((ROWS, LISTED, BLK, BLK), jnp.bfloat16),
+            pltpu.SMEM((LISTED, ROWS), jnp.int32),
+            pltpu.SMEM((ROWS,), jnp.int32),
+            pltpu.SMEM((3, 4, ROWS), jnp.int32),
+            pltpu.VMEM((ROWS, 32, BLK), jnp.bfloat16),
+            dma((4,)),
+            pltpu.VMEM((ROWS + 1, LISTED, BLK, BLK), jnp.bfloat16),
             kept,
             kept,
             kept,
@@ -390,12 +477,14 @@
             landing,
             pltpu.VMEM((ROWS, BLK, BLK), jnp.float32),
             pltpu.VMEM((ROWS, 1, 3 * BLK), jnp.int32),
-            pltpu.VMEM((3, ROWS * BLK, BLK), jnp.bfloat16),
+            pltpu.VMEM((ROWS, BLK, WIDTH), jnp.float32),
             pltpu.SMEM((1, 2, GROUP), jnp.int32),
             pltpu.SMEM((1, 2, GROUP), jnp.int32),
             index,
             index,
             index,
+            pltpu.SMEM((ROWS,), jnp.int32),
+            pltpu.SMEM((ROWS,), jnp.int32),
             dma,
             dma((2, SLOTS)),
             dma((2, SLOTS)),
@@ -403,9 +492,8 @@
             dma((2,)),
             dma((3, 2 * GROUP)),
             dma((3, 2 * GROUP)),
-            dma((3,)),
         ],
-        compiler_params=pltpu.CompilerParams(collective_id=0, has_side_effects=True, vmem_limit_bytes=48 << 20),
+        compiler_params=pltpu.CompilerParams(collective_id=0, has_side_effects=True, vmem_limit_bytes=60 << 20),
         cost_estimate=pl.CostEstimate(flops=10_000_000_000, bytes_accessed=16_000_000, transcendentals=0),
     )(a_cols.T, owner, p_mask.transpose(1, 2, 0), ghost_send, blocks, near_null)
     return result.transpose(1, 0, 2)

time: 99.6 us -> 91 us (0.914)
  local copies, waits for them, and re-layouts: 6.92 us -> 1.67 us
  Pallas kernels: 92.4 us -> 89.1 us
    unnamed x13 -> x1, local copies, waits for them, and re-layouts: 6.92 us -> 1.67 us
    pallas_call x1, Pallas kernels: 92.4 us -> 89.1 us  [per_device(): pl.pallas_call(kernel, out_shape=pltpu.VMEM((3, ROWS * BLK, BLK), jnp.bfl...]
where the time goes in v2:
time: 91 us; the launch traced here: 90.8 us
  Pallas kernels  89.1 us (98%)
  local copies, waits for them, and re-layouts  1.67 us (2%)
    pallas_call x1, Pallas kernels, per_device(): pl.pallas_call(kernel, out_shape=pltpu.VMEM((3, ROWS * BLK, BLK), jnp.bfl...  89.1 us

profile of v2, /device:TPU:2, one launch (start us, length us, event | category | flops | bytes accessed | tf_op | source)
XLA Modules:
  0.0 90.8 jit_solution(3059431538299528029)
XLA Ops:
  0.0 89.1 %shard_map.64 = bf16[3,4096,128]{2,1,0:T(8,128)(2,1)S(1)} custom-call(s32[8,32]{1,0:T(8,128)} %bitcast.5, s32[32]{0:T(128)} %owner_in.1, s32[3,4,32]{2,1,0:T(4,128)} %bitcast.4, s32[1,2,8]{2,1,0:T(2,128)} %lists.1, bf16[8,8,128,128]{3,2,1,0:T(8,128)(2,1)} %blocks.1, bf16[32,32,128]{2,1,0:T(8,128)(2,1)} %vectors_in.1), custom_call_target="tpu_custom_call" | custom-call | flops 10000000000 | bytes 16000000 | tf_op jit(solution)/shard_map/pallas_call | solution.py:460
  89.1 1.7 %copy.8 = bf16[4096,3,128]{2,0,1:T(8,128)(2,1)} copy(bf16[4096,3,128]{2,0,1:T(8,128)(2,1)S(1)} %bitcast.3) | data formatting | bytes 6291456

commit v3 on v2

--- a/solution.py
+++ b/solution.py
@@ -14,6 +14,7 @@
 WIDTH = 2 * BLK
 EMPTY = ROWS + 2 * GROUP
 SLOTS = 12
+AHEAD = 4
 MESH = pl.DeviceIdType.MESH
 
 
@@ -24,11 +25,17 @@
     return group * GROUP + jnp.where(group < 2, place, GROUP - 1 - place)
 
 
+def is_forward(slot):
+    return (slot == 4) | (slot == 6) | (slot >= SLOTS - 2)
+
+
 def slot_row(sender, slot, leftward):
-    forwards = slot >= GROUP
+    forwards = is_forward(slot)
     source = lax.rem(sender + jnp.where(leftward, 1, COL - 1), COL)
     group = jnp.where(forwards, source, sender)
-    position = jnp.where(forwards, slot - GROUP, slot)
+    own = jnp.where(slot < 4, slot, jnp.where(slot == 5, 4, slot - 2))
+    passed = jnp.where(slot < SLOTS - 2, slot // 2 - 2, slot - GROUP)
+    position = jnp.where(forwards, passed, own)
     return sent_row(group, position, leftward)
 
 
@@ -97,7 +104,7 @@
             device_id_type=MESH,
         )
 
-    for slot in range(GROUP):
+    for slot in range(AHEAD):
         for leftward in (False, True):
             gather_copy(slot, leftward, True).start()
     own_copy.start()
@@ -150,14 +157,15 @@
 
     late_pair = sent_row(lax.rem(me + 2, COL), SLOTS - GROUP - 1, False) // 2
     late_a, late_b = 2 * late_pair, 2 * late_pair + 1
-    edge_pair = jnp.where(me == 2, ROWS // 2 - 1, 0)
+    edge_pair = jnp.where(me == 2, ROWS // 2 - 2, 0)
 
     def other_pair(number, turn):
         first = lax.rem(late_pair + turn, ROWS // 2)
         second = lax.rem(edge_pair + turn, ROWS // 2)
-        low, high = jnp.minimum(first, second), jnp.maximum(first, second)
-        place = number + jnp.where(number >= low, 1, 0)
-        place = place + jnp.where(place >= high, 1, 0)
+        low = jnp.minimum(first, second)
+        high = jnp.maximum(first, second)
+        place = number + jnp.where(number >= low, jnp.where(second < first, 2, 1), 0)
+        place = place + jnp.where(place >= high, jnp.where(second < first, 1, 2), 0)
         return lax.rem(place + ROWS // 2 - turn, ROWS // 2)
 
     lane = lax.broadcasted_iota(jnp.int32, (1, BLK), 1) // 32
@@ -290,16 +298,30 @@
     p1[late_a] = jnp.zeros((BLK, WIDTH), jnp.bfloat16)
     p1[late_b] = jnp.zeros((BLK, WIDTH), jnp.bfloat16)
 
-    @pl.loop(0, SLOTS - GROUP)
+    def send_slot(slot):
+        @pl.when(is_forward(slot))
+        def _():
+            gather_copy(slot, False, False).start()
+            gather_copy(slot, True, False).start()
+
+        @pl.when(jnp.logical_not(is_forward(slot)))
+        def _():
+            gather_copy(slot, False, True).start()
+            gather_copy(slot, True, True).start()
+
+    @pl.loop(0, SLOTS - 1)
     def _(slot):
         rows = receive(slot)
-        gather_copy(slot + GROUP, False, False).start()
-        gather_copy(slot + GROUP, True, False).start()
+
+        @pl.when(slot + AHEAD < SLOTS - 2)
+        def _():
+            send_slot(slot + AHEAD)
+
         first_sweep(*rows)
 
-    @pl.loop(SLOTS - GROUP, SLOTS - 1)
-    def _(slot):
-        first_sweep(*receive(slot))
+        @pl.when((slot >= SLOTS - 4) & (slot < SLOTS - 2))
+        def _():
+            send_slot(slot + 2)
 
     def take_ghost(source, landed, sweep, place):
         @pl.when(place < GROUP)
@@ -325,16 +347,16 @@
                 finish(number - 1)
         finish(len(pairs) - 1)
 
-    late_ghost = jnp.where(me == 2, 2 * GROUP - 2, 0)
-    p1[ROWS + late_ghost] = jnp.zeros((BLK, WIDTH), jnp.bfloat16)
-    p1[ROWS + late_ghost + 1] = jnp.zeros((BLK, WIDTH), jnp.bfloat16)
+    late_ghost = jnp.where(me == 2, 2 * GROUP - 4, 0)
+    for i in range(4):
+        p1[ROWS + late_ghost + i] = jnp.zeros((BLK, WIDTH), jnp.bfloat16)
     partial_rows(range(7))
 
-    @pl.loop(0, 2 * GROUP - 2)
+    @pl.loop(0, 2 * GROUP - 4)
     def _(i):
-        take_ghost(p1, land1, 1, i + jnp.where(me == 2, 0, 2))
-
-    partial_rows(range(7, 14))
+        take_ghost(p1, land1, 1, i + jnp.where(me == 2, 0, 4))
+
+    partial_rows(range(7, 13))
     first_sweep(*receive(SLOTS - 1))
 
     send_second = send_ghost(p2, land2, 2)
@@ -372,10 +394,13 @@
 
     corrected_rows(range(4))
     corrected_rows(range(4, 7))
-    corrected_rows(range(7, 14))
-    take_ghost(p1, land1, 1, late_ghost)
-    take_ghost(p1, land1, 1, late_ghost + 1)
-    sweep_rows(p1, p2, [2 * edge_pair, 2 * edge_pair + 1], send_second)
+    corrected_rows(range(7, 13))
+
+    @pl.loop(0, 4)
+    def _(i):
+        take_ghost(p1, land1, 1, late_ghost + i)
+
+    sweep_rows(p1, p2, [2 * edge_pair + i for i in range(4)], send_second)
 
     def put(w, r, value):
         out[w, pl.ds(pl.multiple_of(r * BLK, BLK), BLK), :] = value
@@ -434,12 +459,12 @@
 
     @pl.loop(0, SLOTS)
     def _(slot):
-        @pl.when(slot >= GROUP)
+        @pl.when(is_forward(slot))
         def _():
             gather_copy(slot, False, False).wait_send()
             gather_copy(slot, True, False).wait_send()
 
-        @pl.when(slot < GROUP)
+        @pl.when(jnp.logical_not(is_forward(slot)))
         def _():
             gather_copy(slot, False, True).wait_send()
             gather_copy(slot, True, True).wait_send()

time: 91 us -> 90.9 us (level)
  no operation moved by 1% of the time
where the time goes in v3:
time: 90.9 us; the launch traced here: 90.8 us
  Pallas kernels  89.1 us (98%)
  local copies, waits for them, and re-layouts  1.67 us (2%)
    pallas_call x1, Pallas kernels, per_device(): pl.pallas_call(kernel, out_shape=pltpu.VMEM((3, ROWS * BLK, BLK), jnp.bfl...  89.1 us

profile of v3, /device:TPU:2, one launch (start us, length us, event | category | flops | bytes accessed | tf_op | source)
XLA Modules:
  0.0 90.8 jit_solution(2262681717657244732)
XLA Ops:
  0.0 89.1 %shard_map.64 = bf16[3,4096,128]{2,1,0:T(8,128)(2,1)S(1)} custom-call(s32[8,32]{1,0:T(8,128)} %bitcast.5, s32[32]{0:T(128)} %owner_in.1, s32[3,4,32]{2,1,0:T(4,128)} %bitcast.4, s32[1,2,8]{2,1,0:T(2,128)} %lists.1, bf16[8,8,128,128]{3,2,1,0:T(8,128)(2,1)} %blocks.1, bf16[32,32,128]{2,1,0:T(8,128)(2,1)} %vectors_in.1), custom_call_target="tpu_custom_call" | custom-call | flops 10000000000 | bytes 16000000 | tf_op jit(solution)/shard_map/pallas_call | solution.py:485
  89.1 1.7 %copy.8 = bf16[4096,3,128]{2,0,1:T(8,128)(2,1)} copy(bf16[4096,3,128]{2,0,1:T(8,128)(2,1)S(1)} %bitcast.3) | data formatting | bytes 6291456

commit v4 on v2

--- a/solution.py
+++ b/solution.py
@@ -330,7 +330,7 @@
     p1[ROWS + late_ghost + 1] = jnp.zeros((BLK, WIDTH), jnp.bfloat16)
     partial_rows(range(7))
 
-    @pl.loop(0, 2 * GROUP - 2)
+    @pl.loop(0, 2 * GROUP - 2, unroll=True)
     def _(i):
         take_ghost(p1, land1, 1, i + jnp.where(me == 2, 0, 2))
 
@@ -426,7 +426,7 @@
     def _(number):
         upper = jnp.where(me == 2, number, 1 - number)
 
-        @pl.loop(0, GROUP)
+        @pl.loop(0, GROUP, unroll=True)
         def _(i):
             take_ghost(p2, land2, 2, upper * GROUP + i)
 

time: 91 us -> 91 us (level)
  no operation moved by 1% of the time
where the time goes in v4:
time: 91 us; the launch traced here: 90.8 us
  Pallas kernels  89.1 us (98%)
  local copies, waits for them, and re-layouts  1.67 us (2%)
    pallas_call x1, Pallas kernels, per_device(): pl.pallas_call(kernel, out_shape=pltpu.VMEM((3, ROWS * BLK, BLK), jnp.bfl...  89.1 us

profile of v4, /device:TPU:2, one launch (start us, length us, event | category | flops | bytes accessed | tf_op | source)
XLA Modules:
  0.0 90.8 jit_solution(15045873999765153843)
XLA Ops:
  0.0 89.1 %shard_map.64 = bf16[3,4096,128]{2,1,0:T(8,128)(2,1)S(1)} custom-call(s32[8,32]{1,0:T(8,128)} %bitcast.5, s32[32]{0:T(128)} %owner_in.1, s32[3,4,32]{2,1,0:T(4,128)} %bitcast.4, s32[1,2,8]{2,1,0:T(2,128)} %lists.1, bf16[8,8,128,128]{3,2,1,0:T(8,128)(2,1)} %blocks.1, bf16[32,32,128]{2,1,0:T(8,128)(2,1)} %vectors_in.1), custom_call_target="tpu_custom_call" | custom-call | flops 10000000000 | bytes 16000000 | tf_op jit(solution)/shard_map/pallas_call | solution.py:460
  89.1 1.7 %copy.8 = bf16[4096,3,128]{2,0,1:T(8,128)(2,1)} copy(bf16[4096,3,128]{2,0,1:T(8,128)(2,1)S(1)} %bitcast.3) | data formatting | bytes 6291456
